TPU v7x, 256 devices: a whole 4x4x8 slice. The times are simulated.
256 devices in a mesh: seq: 16 (over z, core), wt: 16 (over x, y).
Axes of the slice: x: 4, y: 4, z: 8, core: 2. Of those that a mesh axis runs over, the one named last changes fastest.
Arguments:
- queries: bfloat16 [8192, 8192], P('seq', 'wt'), may hold values from -6 to 6
- keys_in: bfloat16 [8192, 8192], P('seq', 'wt'), may hold values from -6 to 6
- values_in: bfloat16 [8192, 8192], P('seq', 'wt'), may hold values from -6 to 6
- stream: bfloat16 [8192, 8192], P('seq', 'wt')
- attn_gain: float32 [8192], P('wt'), may hold values from 0.1 to 1.9
- mlp_gain: float32 [8192], replicated, may hold values from 0.1 to 1.9
- up_index: int32 [128, 16], P('wt'), may hold values from 0 to 63, all different within a row
- up_blocks: bfloat16 [128, 16, 128, 128], P('wt'), may hold values from -0.125 to 0.125
- down_index: int32 [128, 16], P('wt'), may hold values from 0 to 63, all different within a row
- down_blocks: bfloat16 [128, 16, 128, 128], P('wt'), may hold values from -0.09375 to 0.09375
Outputs:
- result: bfloat16 [8192, 8192], P('seq', 'wt')
Inputs may be any that keep to these rules, and one draw needn't show every extreme that they name: `up_index`: each row names 16 different feature blocks, and every feature block is named by some row. `down_index`: each row names 16 different output blocks, and every output block is named by some row.
All inputs are finite; a program needn't handle non-finite values.
Results may differ from a plain program's by a relative error of at most 0.013.
Values may be sent and summed in bfloat16 or wider, within the bound.
No kernel may reach another device: no remote copies, remote signals or barrier semaphores. Data moves between devices by JAX's collectives and lax.ppermute only.
A program may use at most 128 MiB of HBM per device.

v0:
```python
import jax
import jax.numpy as jnp
from jax import lax
from jax.sharding import PartitionSpec as P

HEAD = 128
BLK = 128


def carried_in(x, axis, join, neutral):
    place = lax.axis_index(axis)
    gathered = lax.all_gather(x.astype(jnp.bfloat16), axis)
    state = jnp.zeros_like(x) + jnp.asarray(neutral, x.dtype)

    def one(step, state):
        return join(state, lax.dynamic_index_in_dim(gathered, step, 0, False).astype(x.dtype))

    return lax.fori_loop(0, place, one, state)


def feature_map(a):
    return (jax.nn.elu(a.astype(jnp.float32)) + 1.0).astype(jnp.bfloat16)


def add_states(earlier, later):
    return earlier + later


def per_device(
    queries,
    keys_in,
    values_in,
    stream,
    attn_gain,
    mlp_gain,
    up_index,
    up_blocks,
    down_index,
    down_blocks,
):
    rows = queries.shape[0]
    local_cols = queries.shape[1]
    local_heads = local_cols // HEAD
    fq = feature_map(queries).reshape(rows, local_heads, HEAD)
    fk = feature_map(keys_in).reshape(rows, local_heads, HEAD)
    vals = values_in.reshape(rows, local_heads, HEAD)
    causal = jnp.tril(jnp.ones((rows, rows), dtype=bool))
    scores = jnp.einsum("thd,shd->hts", fq, fk, preferred_element_type=jnp.float32)
    scores = jnp.where(causal[None], scores, 0.0).astype(jnp.bfloat16)
    intra = jnp.einsum("hts,shd->thd", scores, vals, preferred_element_type=jnp.float32)
    own_state = jnp.einsum("shd,she->hde", fk, vals, preferred_element_type=jnp.float32)
    empty = jnp.zeros_like(own_state)
    before = carried_in(own_state, "seq", add_states, empty)
    inter = jnp.einsum(
        "thd,hde->the", fq.astype(jnp.float32), before, precision=lax.Precision.HIGHEST
    )
    raw = intra + inter
    normal_raw = raw * lax.rsqrt(jnp.mean(raw * raw, axis=-1, keepdims=True) + 1e-06)
    attn = normal_raw.reshape(rows, local_cols) * attn_gain
    mid = (stream.astype(jnp.float32) + attn).astype(jnp.bfloat16)
    width = mlp_gain.shape[0]
    whole = lax.all_gather(mid, "wt", axis=1, tiled=True)
    whole_f = whole.astype(jnp.float32)
    scale = lax.rsqrt(jnp.mean(whole_f * whole_f, axis=-1, keepdims=True) + 1e-06)
    normed = (whole_f * scale * mlp_gain).astype(jnp.bfloat16)
    tiles = normed.reshape(rows, width // BLK, BLK)
    own_blocks = up_blocks.shape[0]
    picks = jnp.take(tiles, up_index.reshape(-1), axis=1)
    picks = picks.reshape(rows, own_blocks, up_index.shape[1], BLK)
    upper = jnp.einsum("lckd,ckde->lce", picks, up_blocks, preferred_element_type=jnp.float32)
    act = jax.nn.silu(upper).astype(jnp.bfloat16)
    parts = jnp.einsum("lrd,rkde->rkle", act, down_blocks, preferred_element_type=jnp.float32)
    parts = parts.reshape(-1, rows, BLK)
    summed = jax.ops.segment_sum(parts, down_index.reshape(-1), num_segments=width // BLK)
    partial_sum = summed.astype(jnp.bfloat16)
    mine = lax.psum_scatter(partial_sum, "wt", scatter_dimension=0, tiled=True).astype(jnp.float32)
    down = jnp.transpose(mine, (1, 0, 2)).reshape(rows, local_cols)
    return (mid.astype(jnp.float32) + down).astype(jnp.bfloat16)


def solution(mesh):
    placed = (
        P("seq", "wt"),
        P("seq", "wt"),
        P("seq", "wt"),
        P("seq", "wt"),
        P("wt"),
        P(),
        P("wt", None),
        P("wt", None, None, None),
        P("wt", None),
        P("wt", None, None, None),
    )
    return jax.shard_map(
        per_device, mesh=mesh, in_specs=placed, out_specs=P("seq", "wt"), check_vma=False
    )
```

profile of v0, /device:TPU:2, one launch (start us, length us, event | category | flops | bytes accessed | tf_op | source)
XLA Modules:
  0.0 391.9 jit_solution(10710767317259980740)
XLA Ops:
  6.5 0.0 copy-start
  6.5 0.0 copy-start.8
  6.5 0.0 all-gather.6.cloned.1.call-start
  6.5 1.6 fusion.27
  8.1 0.2 copy.49
  8.4 0.0 copy-done
  8.4 0.9 convolution_convert_fusion
  9.3 0.0 all-gather.6.cloned.1.call-update
  9.3 0.0 all-gather.4.cloned.1.call-start
  9.4 1.3 copy.35
  10.6 0.0 copy-start.7
  10.7 0.1 iota_compare_fusion
  10.7 41.4 %all-gather.6.cloned.1.call-done = bf16[64,128,128]{2,1,0:T(8,128)(2,1)} async-done(((bf16[4,128,128]{2,1,0:T(8,128)(2,1)}), bf16[64,128,128]{2,1,0:T(8,128)(2,1)}) %all-gather.6.cloned.1.call-update) | async-done | bytes 2097168 | tf_op jit(solution)/shard_map/all_gather | solution.py:12
  52.2 0.0 copy-start.6
  52.2 0.0 copy-start.5
  52.2 0.0 copy-done.8
  52.2 1.9 convolution_bitcast_fusion
  54.2 2.8 multiply_reduce_fusion
  57.0 0.0 copy-start.4
  57.1 0.1 broadcast_multiply_fusion
  57.2 0.0 copy-done.7
  57.2 1.0 fusion.30
  58.2 0.0 all-gather.4.cloned.1.call-update
  58.2 0.2 reduce-scatter.2.cloned.1.call-start
  58.5 0.0 copy-done.6
  58.5 0.1 reshape.114
  58.6 0.0 copy-done.5
  58.6 0.1 reshape.96
  58.7 87.3 %all-gather.4.cloned.1.call-done = bf16[512,8192]{0,1:T(8,128)(2,1)} async-done(((bf16[512,512]{0,1:T(8,128)(2,1)}), bf16[512,8192]{0,1:T(8,128)(2,1)}) %all-gather.4.cloned.1.call-update) | async-done | bytes 8388624 | tf_op jit(solution)/shard_map/all_gather | solution.py:62
  146.0 0.0 copy-start.2
  146.0 5.3 %fusion = f32[512]{0:T(512)S(1)} fusion(bf16[512,8192]{0,1:T(8,128)(2,1)} %all-gather.4.cloned.1.call-done), kind=kLoop, calls=%fused_computation.5 | loop fusion | flops 12582400 | bytes 8390656 | tf_op jit(solution)/shard_map/reduce_sum | solution.py:64
  151.3 0.0 copy-done.4
  151.3 0.4 copy-done.2
  151.7 4.4 %fusion.2 = bf16[512,8192]{0,1:T(8,128)(2,1)} fusion(bf16[512,8192]{0,1:T(8,128)(2,1)S(1)} %copy-done.2, f32[8192]{0:T(1024)S(1)} %copy-done.4, f32[512]{0:T(512)S(1)} %add_rsqrt_fusion.1), kind=kLoop, calls=%fused_computation.7 | loop fusion | flops 16777216 | bytes 16812032 | tf_op jit(solution)/shard_map/convert_element_type | solution.py:65
  156.1 12.0 %copy.43 = bf16[512,64,128]{2,0,1:T(8,128)(2,1)} copy(bf16[512,64,128]{0,2,1:T(8,128)(2,1)} %bitcast.96) | data formatting | bytes 16777216 | tf_op jit(solution)/shard_map/reshape | solution.py:66
  168.1 11.8 %gather_fusion = bf16[128,512,128]{2,1,0:T(8,128)(2,1)} fusion(bf16[512,64,128]{2,0,1:T(8,128)(2,1)} %copy.43, s32[1024]{0:T(1024)S(1)} %pad_clamp_fusion), kind=kCustom, calls=%fused_computation | custom fusion | bytes 33554944 | tf_op jit(solution)/shard_map/jit(_take)/gather | solution.py:68
  179.9 21.8 %fusion.20 = f32[8,512,16,128]{3,1,2,0:T(8,128)} fusion(bf16[8,16,128,128]{3,2,1,0:T(8,128)(2,1)} %param.21, bf16[8,16,128,128]{3,2,1,0:T(8,128)(2,1)} %param.19, bf16[512,8,16,128]{3,0,2,1:T(8,128)(2,1)} %bitcast.95, pred[8,16]{1,0:T(8,128)(4,1)S(1)} %compare_and_fusion), kind=kOutput, calls=%fused_computation.28 | convolution fusion | flops 4305977344 | bytes 58720384 | tf_op jit(solution)/shard_map/lrd,rkde->rkle/dot_general | solution.py:72
  201.7 7.8 %broadcast_in_dim.43 = f32[64,512,128]{2,1,0:T(8,128)} broadcast(f32[]{:T(128)} %constant.27.clone.1), dimensions={} | broadcast | bytes 16777220 | tf_op jit(solution)/shard_map/broadcast_in_dim | solution.py:74
  209.5 73.8 %scatter_fusion = f32[64,512,128]{2,1,0:T(8,128)} fusion(f32[64,512,128]{2,1,0:T(8,128)} %broadcast_in_dim.43, s32[128]{0:T(128)S(1)} %reshape.114, f32[128,512,128]{2,1,0:T(8,128)} %bitcast.94), kind=kCustom, calls=%fused_computation.1 | custom fusion | flops 8388608 | bytes 100663808 | tf_op jit(solution)/shard_map/scatter-add | solution.py:74
  283.3 0.0 copy-start.1
  283.3 9.3 %convert_element_type.62 = bf16[64,512,128]{2,1,0:T(8,128)(2,1)} convert(f32[64,512,128]{2,1,0:T(8,128)} %scatter_fusion) | non-fusion elementwise | flops 4194304 | bytes 25165824 | tf_op jit(solution)/shard_map/convert_element_type | solution.py:75
  292.6 0.0 copy-start.3
  292.6 0.0 reduce-scatter.2.cloned.1.call-update
  292.6 90.1 %reduce-scatter.2.cloned.1.call-done = bf16[4,512,128]{2,1,0:T(8,128)(2,1)} async-done(((bf16[64,512,128]{2,1,0:T(8,128)(2,1)}), bf16[4,512,128]{2,1,0:T(8,128)(2,1)}) %reduce-scatter.2.cloned.1.call-update) | async-done | bytes 524304 | tf_op jit(solution)/shard_map/reduce_scatter | solution.py:76
  382.7 1.1 convert_bitcast_fusion
  383.8 0.3 copy.44
  384.2 0.0 copy-done.3
  384.2 0.2 fusion.28
  384.4 1.0 copy.45
  385.4 0.0 copy-done.1
  (7 shorter events, 0.1 us)
Async XLA Ops:
  6.5 1.8 copy-start
  6.5 45.7 %copy-start.8 = (bf16[512,512]{1,0:T(8,128)(2,1)S(1)}, bf16[512,512]{1,0:T(8,128)(2,1)}, u32[]{:S(2)}) copy-start(bf16[512,512]{1,0:T(8,128)(2,1)} %param.12) | copy-start | bytes 1572868
  6.5 45.6 %all-gather.6.cloned.1.call-start = ((), (), s32[]{:S(2)}) async-start(), calls=%async_computation.3 | async-start | bytes 2228224 | tf_op jit(solution)/shard_map/all_gather | solution.py:12
  9.3 136.6 %all-gather.4.cloned.1.call-start = ((), (), s32[]{:S(2)}) async-start(), calls=%async_computation.1 | async-start | bytes 8912896 | tf_op jit(solution)/shard_map/all_gather | solution.py:62
  10.6 46.6 %copy-start.7 = (f32[512]{0:T(512)S(1)}, f32[512]{0:T(512)}, u32[]{:S(2)}) copy-start(f32[512]{0:T(512)} %param.16) | copy-start | bytes 6148
  52.2 6.3 %copy-start.6 = (s32[8,16]{1,0:T(8,128)S(1)}, s32[8,16]{1,0:T(8,128)}, u32[]{:S(2)}) copy-start(s32[8,16]{1,0:T(8,128)} %param.20) | copy-start | bytes 1540
  52.2 6.3 %copy-start.5 = (s32[8,16]{1,0:T(8,128)S(1)}, s32[8,16]{1,0:T(8,128)}, u32[]{:S(2)}) copy-start(s32[8,16]{1,0:T(8,128)} %param.18) | copy-start | bytes 1540
  57.0 94.2 %copy-start.4 = (f32[8192]{0:T(1024)S(1)}, f32[8192]{0:T(1024)}, u32[]{:S(2)}) copy-start(f32[8192]{0:T(1024)} %param.17) | copy-start | bytes 98308
  58.2 324.5 %reduce-scatter.2.cloned.1.call-start = ((), (), s32[]{:S(2)}) async-start(), calls=%async_computation.2 | async-start | bytes 8912896 | tf_op jit(solution)/shard_map/reduce_scatter | solution.py:76
  146.0 5.8 %copy-start.2 = (bf16[512,8192]{0,1:T(8,128)(2,1)S(1)}, bf16[512,8192]{0,1:T(8,128)(2,1)}, u32[]{:S(2)}) copy-start(bf16[512,8192]{0,1:T(8,128)(2,1)} %all-gather.4.cloned.1.call-done) | copy-start | bytes 25165828
  283.3 102.1 %copy-start.1 = (bf16[512,512]{1,0:T(8,128)(2,1)S(1)}, bf16[512,512]{1,0:T(8,128)(2,1)}, u32[]{:S(2)}) copy-start(bf16[512,512]{1,0:T(8,128)(2,1)} %param.14) | copy-start | bytes 1572868
  292.6 91.6 %copy-start.3 = (bf16[512,512]{0,1:T(8,128)(2,1)S(1)}, bf16[512,512]{0,1:T(8,128)(2,1)}, u32[]{:S(2)}) copy-start(bf16[512,512]{0,1:T(8,128)(2,1)} %fusion.30) | copy-start | bytes 1572868
Sparse Core Ops, SparseCore 0:
  9.5 42.6 all-gather.5
  58.4 87.5 all-gather.3
  292.7 89.9 reduce-scatter.1
where the time goes:
time: 393 us; the launch traced here: 392 us
  waiting for transfers between devices  219 us (56%)
  other arithmetic  96.8 us (25%)
  local copies, waits for them, and re-layouts  35.1 us (9%)
  matrix products  27.6 us (7%)
  between operations  13.3 us (3%)
    reduce_scatter x1, waiting for transfers between devices, per_device(): lax.psum_scatter(partial_sum, 'wt', scatter_dimension=0, tiled=True)  90.1 us
    all_gather x1, waiting for transfers between devices, per_device(): whole = lax.all_gather(mid, 'wt', axis=1, tiled=True)  87.3 us
    scatter-add x1, other arithmetic, per_device(): jax.ops.segment_sum(parts, down_index.reshape(-1), num_segments=width //...  73.8 us
    all_gather x1, waiting for transfers between devices, carried_in(): gathered = lax.all_gather(x.astype(jnp.bfloat16), axis)  41.4 us
    dot_general x1, matrix products, per_device(): jnp.einsum('lrd,rkde->rkle', act, down_blocks, preferred_element_type=jnp...  21.8 us
    reshape x1, local copies, waits for them, and re-layouts, per_device(): tiles = normed.reshape(rows, width // BLK, BLK)  12 us
    gather x1, local copies, waits for them, and re-layouts, per_device(): picks = jnp.take(tiles, up_index.reshape(-1), axis=1)  11.8 us
    convert_element_type x1, other arithmetic, per_device(): partial_sum = summed.astype(jnp.bfloat16)  9.25 us
  transfers between devices with their start and end apart: 3, of which 3 were waited for; matrix products, arithmetic and copies ran while one was open for 0% of the time, Pallas kernels for 0%

commit v1 on v0

--- a/solution.py
+++ b/solution.py
@@ -59,7 +59,9 @@
     attn = normal_raw.reshape(rows, local_cols) * attn_gain
     mid = (stream.astype(jnp.float32) + attn).astype(jnp.bfloat16)
     width = mlp_gain.shape[0]
-    whole = lax.all_gather(mid, "wt", axis=1, tiled=True)
+    whole = jnp.concatenate(
+        lax.all_to_all(jnp.stack([mid] * lax.axis_size("wt")), "wt", 0, 0), axis=1
+    )
     whole_f = whole.astype(jnp.float32)
     scale = lax.rsqrt(jnp.mean(whole_f * whole_f, axis=-1, keepdims=True) + 1e-06)
     normed = (whole_f * scale * mlp_gain).astype(jnp.bfloat16)

time: 393 us -> 504 us (1.28)
  waiting for transfers between devices: 219 us -> 297 us
  other arithmetic: 96.8 us -> 113 us
  local copies, waits for them, and re-layouts: 35.1 us -> 44 us
  starting transfers between devices: 0.27 us -> 7.63 us
    all_to_all x0 -> x1, waiting for transfers between devices: none -> 107 us  [per_device(): lax.all_to_all(jnp.stack([mid] * lax.axis_size('wt')), 'wt', 0, 0)]
    all_gather x1 -> x0, waiting for transfers between devices: 87.3 us -> none  [per_device(): whole = lax.all_gather(mid, 'wt', axis=1, tiled=True)]
    reduce_scatter x1, waiting for transfers between devices: 90.1 us -> 149 us  [per_device(): lax.psum_scatter(partial_sum, 'wt', scatter_dimension=0, tiled=True)]
    convert_element_type x0 -> x1, local copies, waits for them, and re-layouts: none -> 17.4 us  [per_device(): whole_f = whole.astype(jnp.float32)]
    reshape x1 -> x0, local copies, waits for them, and re-layouts: 12 us -> none  [per_device(): tiles = normed.reshape(rows, width // BLK, BLK)]
    convert_element_type x0 -> x1, other arithmetic: none -> 11.4 us  [per_device(): whole_f = whole.astype(jnp.float32)]
    all_to_all x0 -> x1, starting transfers between devices: none -> 7.41 us  [per_device(): lax.all_to_all(jnp.stack([mid] * lax.axis_size('wt')), 'wt', 0, 0)]
    convert_element_type x1, other arithmetic: 4.35 us -> 10 us  [per_device(): normed = (whole_f * scale * mlp_gain).astype(jnp.bfloat16)]
where the time goes in v1:
time: 504 us; the launch traced here: 503 us
  waiting for transfers between devices  297 us (59%)
  other arithmetic  113 us (22%)
  local copies, waits for them, and re-layouts  44 us (9%)
  matrix products  27.6 us (5%)
  between operations  13.5 us (3%)
  starting transfers between devices  7.63 us (2%)
    reduce_scatter x1, waiting for transfers between devices, per_device(): lax.psum_scatter(partial_sum, 'wt', scatter_dimension=0, tiled=True)  149 us
    all_to_all x1, waiting for transfers between devices, per_device(): lax.all_to_all(jnp.stack([mid] * lax.axis_size('wt')), 'wt', 0, 0)  107 us
    scatter-add x1, other arithmetic, per_device(): jax.ops.segment_sum(parts, down_index.reshape(-1), num_segments=width //...  73.6 us
    all_gather x1, waiting for transfers between devices, carried_in(): gathered = lax.all_gather(x.astype(jnp.bfloat16), axis)  41.5 us
    dot_general x1, matrix products, per_device(): jnp.einsum('lrd,rkde->rkle', act, down_blocks, preferred_element_type=jnp...  21.9 us
    convert_element_type x1, local copies, waits for them, and re-layouts, per_device(): whole_f = whole.astype(jnp.float32)  17.4 us
    gather x1, local copies, waits for them, and re-layouts, per_device(): picks = jnp.take(tiles, up_index.reshape(-1), axis=1)  11.8 us
    convert_element_type x1, other arithmetic, per_device(): whole_f = whole.astype(jnp.float32)  11.4 us
  transfers between devices with their start and end apart: 3, of which 3 were waited for; matrix products, arithmetic and copies ran while one was open for 0% of the time, Pallas kernels for 0%

profile of v1, /device:TPU:2, one launch (start us, length us, event | category | flops | bytes accessed | tf_op | source)
XLA Modules:
  0.0 503.0 jit_solution(2217390505003659784)
XLA Ops:
  6.5 0.0 copy-start
  6.5 0.0 copy-start.6
  6.5 0.0 all-gather.3.cloned.1.call-start
  6.5 1.6 fusion.24
  8.1 0.2 copy.50
  8.4 0.0 copy-done
  8.4 0.9 convolution_convert_fusion
  9.3 0.0 all-gather.3.cloned.1.call-update
  9.3 1.3 copy.36
  10.6 0.0 copy-start.5
  10.6 0.1 iota_compare_fusion
  10.7 41.5 %all-gather.3.cloned.1.call-done = bf16[64,128,128]{2,1,0:T(8,128)(2,1)} async-done(((bf16[4,128,128]{2,1,0:T(8,128)(2,1)}), bf16[64,128,128]{2,1,0:T(8,128)(2,1)}) %all-gather.3.cloned.1.call-update) | async-done | bytes 2097168 | tf_op jit(solution)/shard_map/all_gather | solution.py:12
  52.2 0.0 copy-done.6
  52.2 2.0 convolution_bitcast_fusion
  54.2 2.8 multiply_reduce_fusion.1
  57.0 0.1 broadcast_multiply_fusion
  57.2 0.0 copy-done.5
  57.2 0.2 fusion.27
  57.4 4.0 stack.2
  61.4 0.0 copy-start.4
  61.4 0.0 copy-start.3
  61.4 7.4 %all-to-all-start = ((bf16[16,512,512]{1,2,0:T(8,128)(2,1)}), bf16[16,512,512]{1,2,0:T(8,128)(2,1)}, u32[]{:S(2)}, u32[]{:S(2)}) async-start(bf16[16,512,512]{1,2,0:T(8,128)(2,1)} %stack.2), calls=%async_computation | async-start | bytes 16777216 | tf_op jit(solution)/shard_map/all_to_all | solution.py:63
  68.8 0.2 reduce-scatter.2.cloned.1.call-start
  69.1 0.0 copy-done.4
  69.1 0.1 reshape.129
  69.2 0.0 copy-done.3
  69.2 0.1 reshape.110
  69.3 106.8 %all-to-all-done = bf16[16,512,512]{1,2,0:T(8,128)(2,1)} async-done(((bf16[16,512,512]{1,2,0:T(8,128)(2,1)}), bf16[16,512,512]{1,2,0:T(8,128)(2,1)}, u32[]{:S(2)}, u32[]{:S(2)}) %all-to-all-start) | async-done | bytes 8388640 | tf_op jit(solution)/shard_map/all_to_all | solution.py:63
  176.1 5.2 %multiply_reduce_fusion = f32[512]{0:T(512)S(1)} fusion(bf16[16,512,512]{1,2,0:T(8,128)(2,1)} %all-to-all-done), kind=kLoop, calls=%fused_computation.6 | loop fusion | flops 12582400 | bytes 8390656 | tf_op jit(solution)/shard_map/reduce_sum | solution.py:66
  181.2 11.4 %convert_element_type.81 = f32[16,512,512]{1,2,0:T(8,128)} convert(bf16[16,512,512]{1,2,0:T(8,128)(2,1)} %all-to-all-done) | non-fusion elementwise | flops 4194304 | bytes 25165824 | tf_op jit(solution)/shard_map/convert_element_type | solution.py:65
  192.7 0.0 copy-start.2
  192.7 17.4 %copy.44 = f32[512,64,128]{2,0,1:T(8,128)} copy(f32[512,64,128]{0,2,1:T(8,128)} %bitcast.98) | data formatting | bytes 33554432 | tf_op jit(solution)/shard_map/convert_element_type | solution.py:65
  210.1 0.0 copy-done.2
  210.1 10.0 %multiply_convert_fusion = bf16[512,64,128]{2,0,1:T(8,128)(2,1)} fusion(f32[512,64,128]{2,0,1:T(8,128)} %copy.44, f32[64,128]{1,0:T(8,128)S(1)} %bitcast.103, f32[512]{0:T(512)S(1)} %add_rsqrt_fusion.1), kind=kLoop, calls=%fused_computation.5 | loop fusion | flops 12582912 | bytes 25200640 | tf_op jit(solution)/shard_map/convert_element_type | solution.py:67
  220.1 11.8 %gather_fusion = bf16[128,512,128]{2,1,0:T(8,128)(2,1)} fusion(bf16[512,64,128]{2,0,1:T(8,128)(2,1)} %multiply_convert_fusion, s32[1024]{0:T(1024)S(1)} %pad_clamp_fusion), kind=kCustom, calls=%fused_computation | custom fusion | bytes 33554944 | tf_op jit(solution)/shard_map/jit(_take)/gather | solution.py:70
  231.9 21.9 %fusion.17 = f32[8,512,16,128]{3,1,2,0:T(8,128)} fusion(bf16[8,16,128,128]{3,2,1,0:T(8,128)(2,1)} %param.21, bf16[8,16,128,128]{3,2,1,0:T(8,128)(2,1)} %param.19, bf16[512,8,16,128]{3,0,2,1:T(8,128)(2,1)} %bitcast.99, pred[8,16]{1,0:T(8,128)(4,1)S(1)} %compare_and_fusion), kind=kOutput, calls=%fused_computation.25 | convolution fusion | flops 4305977344 | bytes 58720384 | tf_op jit(solution)/shard_map/lrd,rkde->rkle/dot_general | solution.py:74
  253.7 7.8 %broadcast_in_dim.43 = f32[64,512,128]{2,1,0:T(8,128)} broadcast(f32[]{:T(128)} %constant.27.clone.1), dimensions={} | broadcast | bytes 16777220 | tf_op jit(solution)/shard_map/broadcast_in_dim | solution.py:76
  261.5 73.6 %scatter_fusion = f32[64,512,128]{2,1,0:T(8,128)} fusion(f32[64,512,128]{2,1,0:T(8,128)} %broadcast_in_dim.43, s32[128]{0:T(128)S(1)} %reshape.129, f32[128,512,128]{2,1,0:T(8,128)} %bitcast.97), kind=kCustom, calls=%fused_computation.1 | custom fusion | flops 8388608 | bytes 100663808 | tf_op jit(solution)/shard_map/scatter-add | solution.py:76
  335.1 0.0 copy-start.1
  335.1 9.3 %convert_element_type.77 = bf16[64,512,128]{2,1,0:T(8,128)(2,1)} convert(f32[64,512,128]{2,1,0:T(8,128)} %scatter_fusion) | non-fusion elementwise | flops 4194304 | bytes 25165824 | tf_op jit(solution)/shard_map/convert_element_type | solution.py:77
  344.4 0.0 reduce-scatter.2.cloned.1.call-update
  344.4 149.1 %reduce-scatter.2.cloned.1.call-done = bf16[4,512,128]{2,1,0:T(8,128)(2,1)} async-done(((bf16[64,512,128]{2,1,0:T(8,128)(2,1)}), bf16[4,512,128]{2,1,0:T(8,128)(2,1)}) %reduce-scatter.2.cloned.1.call-update) | async-done | bytes 524304 | tf_op jit(solution)/shard_map/reduce_scatter | solution.py:78
  493.5 1.1 convert_bitcast_fusion
  494.6 0.3 copy.45
  494.9 0.2 fusion.25
  495.1 1.0 copy.46
  496.1 0.0 copy-done.1
  (7 shorter events, 0.1 us)
Async XLA Ops:
  6.5 1.8 copy-start
  6.5 45.7 %copy-start.6 = (bf16[512,512]{1,0:T(8,128)(2,1)S(1)}, bf16[512,512]{1,0:T(8,128)(2,1)}, u32[]{:S(2)}) copy-start(bf16[512,512]{1,0:T(8,128)(2,1)} %param.12) | copy-start | bytes 1572868
  6.5 45.6 %all-gather.3.cloned.1.call-start = ((), (), s32[]{:S(2)}) async-start(), calls=%async_computation.3 | async-start | bytes 2228224 | tf_op jit(solution)/shard_map/all_gather | solution.py:12
  10.6 46.6 %copy-start.5 = (f32[512]{0:T(512)S(1)}, f32[512]{0:T(512)}, u32[]{:S(2)}) copy-start(f32[512]{0:T(512)} %param.16) | copy-start | bytes 6148
  61.4 7.6 %copy-start.4 = (s32[8,16]{1,0:T(8,128)S(1)}, s32[8,16]{1,0:T(8,128)}, u32[]{:S(2)}) copy-start(s32[8,16]{1,0:T(8,128)} %param.20) | copy-start | bytes 1540
  61.4 7.7 %copy-start.3 = (s32[8,16]{1,0:T(8,128)S(1)}, s32[8,16]{1,0:T(8,128)}, u32[]{:S(2)}) copy-start(s32[8,16]{1,0:T(8,128)} %param.18) | copy-start | bytes 1540
  61.4 114.6 %all-to-all-start = ((bf16[16,512,512]{1,2,0:T(8,128)(2,1)}), bf16[16,512,512]{1,2,0:T(8,128)(2,1)}, u32[]{:S(2)}, u32[]{:S(2)}) async-start(bf16[16,512,512]{1,2,0:T(8,128)(2,1)} %stack.2), calls=%async_computation | async-start | bytes 16777216 | tf_op jit(solution)/shard_map/all_to_all | solution.py:63
  68.8 424.6 %reduce-scatter.2.cloned.1.call-start = ((), (), s32[]{:S(2)}) async-start(), calls=%async_computation.2 | async-start | bytes 8912896 | tf_op jit(solution)/shard_map/reduce_scatter | solution.py:78
  192.7 17.4 %copy-start.2 = (f32[8192]{0:T(1024)S(1)}, f32[8192]{0:T(1024)}, u32[]{:S(2)}) copy-start(f32[8192]{0:T(1024)} %param.17) | copy-start | bytes 98308
  335.1 161.0 %copy-start.1 = (bf16[512,512]{1,0:T(8,128)(2,1)S(1)}, bf16[512,512]{1,0:T(8,128)(2,1)}, u32[]{:S(2)}) copy-start(bf16[512,512]{1,0:T(8,128)(2,1)} %param.14) | copy-start | bytes 1572868
Sparse Core Ops, SparseCore 0:
  9.5 42.6 all-gather.2
  344.5 148.9 reduce-scatter.1
